TPU v7x, 512 devices: a whole 4x8x8 slice. The times are simulated.
512 devices in a mesh: pts: 128 (over y, x, z_hi), band: 4 (over z_lo, core).
Axes of the slice: x: 4, y: 8, z: 8 (z_hi: 4, z_lo: 2; z = z_hi * 2 + z_lo), core: 2. Of those that a mesh axis runs over, the one named last changes fastest.
Arguments:
- orbitals: bfloat16 [2000, 32768], P('band', 'pts'), may hold values from -6 to 6
- partner: int32 [128], P('pts'), may hold values from 0 to 127, as said below
- self_kernel: bfloat16 [32768, 256], P('pts'), may hold values from -0.005859375 to 0.005859375
- pair_kernel: bfloat16 [32768, 256], P('pts'), may hold values from -0.005859375 to 0.005859375
Outputs:
- exchange_out: bfloat16 [2000, 32768], P('band', 'pts')
Inputs may be any that keep to these rules, and one draw needn't show every extreme that they name: partner[p] = (r - p) mod the number of point blocks, for one odd round number r drawn per run; so blocks pair off, and none is its own partner.
All inputs are finite; a program needn't handle non-finite values.
Results may differ from a plain program's by a relative error of at most 0.017.
Values may be sent and summed in bfloat16 or wider, within the bound.
A program may use at most 64 MiB of HBM per device.

v0:
```python
import functools

import jax
import jax.numpy as jnp
from jax import lax
from jax.experimental import pallas as pl
from jax.experimental.pallas import tpu as pltpu
from jax.sharding import PartitionSpec as P

MESH = pl.DeviceIdType.MESH
VMEM = 56 * 1024 * 1024


def swap_kernel(round_number, blocks, orbitals, arrived, send_sem, recv_sem):
    partner = {"pts": lax.rem(round_number + blocks - lax.axis_index("pts"), blocks)}
    barrier = pltpu.get_barrier_semaphore()
    pl.semaphore_signal(barrier, inc=1, device_id=partner, device_id_type=MESH)
    pl.semaphore_wait(barrier, 1)
    copy = pltpu.make_async_remote_copy(
        src_ref=orbitals,
        dst_ref=arrived,
        send_sem=send_sem,
        recv_sem=recv_sem,
        device_id=partner,
        device_id_type=MESH,
    )
    copy.start()
    copy.wait()


def swap(round_number, collective, blocks, orbitals):
    return pl.pallas_call(
        functools.partial(swap_kernel, round_number, blocks),
        out_shape=jax.ShapeDtypeStruct(orbitals.shape, orbitals.dtype),
        in_specs=[pl.BlockSpec(memory_space=pl.ANY)],
        out_specs=pl.BlockSpec(memory_space=pl.ANY),
        scratch_shapes=[pltpu.SemaphoreType.DMA, pltpu.SemaphoreType.DMA],
        compiler_params=pltpu.CompilerParams(
            collective_id=collective, has_side_effects=True, vmem_limit_bytes=VMEM
        ),
    )(orbitals)


def finish_kernel(
    shift,
    blocks,
    groups,
    orbitals,
    swapped,
    self_kernel,
    pair_kernel,
    out,
    own,
    arrived,
    kernels,
    own_t,
    part,
    got,
    dens,
    total,
    local_sem,
    shift_sem,
    rs_send,
    rs_recv,
    ag_send,
    ag_recv,
):
    me = lax.axis_index("pts")
    band = lax.axis_index("band")
    peers = [lax.rem(band + d, groups) for d in range(1, groups)]
    points = own.shape[1]
    rows = points // groups

    loads = [
        pltpu.make_async_copy(orbitals, own, local_sem.at[0]),
        pltpu.make_async_copy(self_kernel, kernels.at[0], local_sem.at[1]),
        pltpu.make_async_copy(pair_kernel, kernels.at[1], local_sem.at[2]),
    ]
    if not shift:
        loads.append(pltpu.make_async_copy(swapped, arrived, local_sem.at[3]))
    for load in loads:
        load.start()

    barrier = pltpu.get_barrier_semaphore()
    for peer in peers:
        pl.semaphore_signal(barrier, inc=1, device_id={"band": peer}, device_id_type=MESH)
    if shift:
        source = {"pts": lax.rem(me + blocks - shift, blocks)}
        pl.semaphore_signal(barrier, inc=1, device_id=source, device_id_type=MESH)
    pl.semaphore_wait(barrier, groups if shift else groups - 1)
    if shift:
        moved = pltpu.make_async_remote_copy(
            src_ref=swapped,
            dst_ref=arrived,
            send_sem=shift_sem.at[0],
            recv_sem=shift_sem.at[1],
            device_id={"pts": lax.rem(me + shift, blocks)},
            device_id_type=MESH,
        )
        moved.start()

    pending = []

    def scatter(stage, block):
        product = jnp.dot(own_t[...], block[...], preferred_element_type=jnp.float32)
        for k in range(groups):
            part[stage, k] = product[k * rows : (k + 1) * rows].astype(jnp.bfloat16)
        copies = []
        for d in range(groups - 1):
            copy = pltpu.make_async_remote_copy(
                src_ref=part.at[stage, peers[d]],
                dst_ref=got.at[stage, d],
                send_sem=rs_send.at[stage, d],
                recv_sem=rs_recv.at[stage, d],
                device_id={"band": peers[d]},
                device_id_type=MESH,
            )
            copy.start()
            copies.append(copy)
        pending.extend(copies)
        return copies

    def gather(stage, arriving):
        value = part[stage, band].astype(jnp.float32)
        for d, copy in enumerate(arriving):
            copy.wait_recv()
            value = value + got[stage, d].astype(jnp.float32)
        dens[stage, band] = value.astype(jnp.bfloat16)
        copies = []
        for d in range(groups - 1):
            copy = pltpu.make_async_remote_copy(
                src_ref=dens.at[stage, band],
                dst_ref=dens.at[stage, band],
                send_sem=ag_send.at[stage, d],
                recv_sem=ag_recv.at[stage, d],
                device_id={"band": peers[d]},
                device_id_type=MESH,
            )
            copy.start()
            copies.append(copy)
        pending.extend(copies)
        return copies

    def apply(stage, block, arriving):
        for copy in arriving:
            copy.wait_recv()
        density = dens[stage].reshape(points, points).astype(jnp.float32)
        weight = (kernels[stage].astype(jnp.float32) * density).astype(jnp.bfloat16)
        return lax.dot_general(
            block[...], weight, (((1,), (1,)), ((), ())), preferred_element_type=jnp.float32
        )

    loads[0].wait()
    own_t[...] = own[...].T
    first = scatter(0, own)
    if shift:
        first = gather(0, first)
        moved.wait_recv()
        second = scatter(1, arrived)
    else:
        loads[3].wait()
        second = scatter(1, arrived)
        first = gather(0, first)
    loads[1].wait()
    loads[2].wait()
    if shift:
        total[...] = apply(0, own, first)
        second = gather(1, second)
    else:
        second = gather(1, second)
        total[...] = apply(0, own, first)
    out[...] = (total[...] + apply(1, arrived, second)).astype(out.dtype)

    if shift:
        moved.wait_send()
    for copy in pending:
        copy.wait_send()


def finish(shift, collective, blocks, groups, orbitals, swapped, self_kernel, pair_kernel):
    bands, points = orbitals.shape
    rows = points // groups
    half = jnp.bfloat16
    dma = pltpu.SemaphoreType.DMA
    return pl.pallas_call(
        functools.partial(finish_kernel, shift, blocks, groups),
        out_shape=jax.ShapeDtypeStruct((bands, points), half),
        in_specs=[pl.BlockSpec(memory_space=pl.ANY)] * 4,
        out_specs=pl.BlockSpec(memory_space=pltpu.VMEM),
        scratch_shapes=[
            pltpu.VMEM((bands, points), half),
            pltpu.VMEM((bands, points), half),
            pltpu.VMEM((2, points, points), half),
            pltpu.VMEM((points, bands), half),
            pltpu.VMEM((2, groups, rows, points), half),
            pltpu.VMEM((2, groups - 1, rows, points), half),
            pltpu.VMEM((2, groups, rows, points), half),
            pltpu.VMEM((bands, points), jnp.float32),
            dma((4,)),
            dma((2,)),
            dma((2, groups - 1)),
            dma((2, groups - 1)),
            dma((2, groups - 1)),
            dma((2, groups - 1)),
        ],
        compiler_params=pltpu.CompilerParams(
            collective_id=collective, has_side_effects=True, vmem_limit_bytes=VMEM
        ),
    )(orbitals, swapped, self_kernel, pair_kernel)


def per_device(blocks, groups, orbitals, partner, self_kernel, pair_kernel):
    shift = max(blocks // 16, 2)
    pairs = shift // 2
    count = blocks // 4
    round_number = lax.rem(partner[0] + lax.axis_index("pts"), blocks)
    bit = lax.rem(round_number // shift, 2)
    index = round_number // (2 * shift) * pairs + lax.rem(round_number, shift) // 2
    swaps = [
        functools.partial(swap, 2 * shift * (k // pairs) + 2 * (k % pairs) + 1, k, blocks)
        for k in range(count)
    ]
    swapped = lax.switch(index, swaps, orbitals)
    return lax.cond(
        bit == 1,
        functools.partial(finish, shift, count, blocks, groups),
        functools.partial(finish, 0, count + 1, blocks, groups),
        orbitals,
        swapped,
        self_kernel,
        pair_kernel,
    )


def solution(mesh):
    return jax.shard_map(
        functools.partial(per_device, mesh.shape["pts"], mesh.shape["band"]),
        mesh=mesh,
        in_specs=(P("band", "pts"), P("pts"), P("pts", None), P("pts", None)),
        out_specs=P("band", "pts"),
        check_vma=False,
    )
```

profile of v0, /device:TPU:447, one launch (start us, length us, event | category | flops | bytes accessed | tf_op | source)
XLA Modules:
  0.0 40.2 jit_solution(4098605480736942097)
XLA Ops:
  0.7 0.0 copy-start
  0.7 0.0 copy-start.1
  0.7 25.3 %conditional.2 = (bf16[500,256]{1,0:T(8,128)(2,1)S(1)}) conditional(s32[]{:T(128)} %clamp.3, bf16[500,256]{1,0:T(8,128)(2,1)} %param.38, bf16[500,256]{1,0:T(8,128)(2,1)} %param.38, bf16[500,256]{1,0:T(8,128)(2,1)} %param.38, bf16[500,256]{1,0:T(8,128)(2,1)} %param.38, bf16[500,256]{1,0:T(8,128)(2,1)} %param.38, ...), branch_computations={%region_0.1_spmd, %region_1.2_spmd, %region_2.3_spmd, %region_3.4_... | conditional | bytes 8 | solution.py:223
  0.8 25.2 %branch_22_fun.1 = bf16[500,256]{1,0:T(8,128)(2,1)S(1)} custom-call(bf16[500,256]{1,0:T(8,128)(2,1)} %orbitals.22), custom_call_target="tpu_custom_call" | custom-call | tf_op jit(solution)/shard_map/cond/branch_22_fun/pallas_call | solution.py:32
  26.0 0.0 copy-done
  26.0 0.0 copy-done.1
  26.1 13.5 %conditional.3 = (bf16[500,256]{1,0:T(8,128)(2,1)S(1)}) conditional(s32[]{:T(128)} %convert_element_type.3, (bf16[500,256]{1,0:T(8,128)(2,1)}, bf16[500,256]{1,0:T(8,128)(2,1)S(1)}, bf16[256,256]{1,0:T(8,128)(2,1)S(1)}, bf16[256,256]{1,0:T(8,128)(2,1)S(1)}) %tuple.146, (bf16[500,256]{1,0:T(8,128)(2,1)}, bf16[500,256]{1,0:T(8,128)(2,1)S(1)}, ...), branch_computations={%region_32.33_spmd, %region_33.34_spmd} | conditional | bytes 8 | solution.py:224
  26.1 13.4 %branch_0_fun.3 = bf16[500,256]{1,0:T(8,128)(2,1)S(1)} custom-call(bf16[500,256]{1,0:T(8,128)(2,1)} %get-tuple-element.89.orbitals, bf16[500,256]{1,0:T(8,128)(2,1)S(1)} %get-tuple-element.90.swapped, bf16[256,256]{1,0:T(8,128)(2,1)S(1)} %get-tuple-element.102.self_kernel, bf16[256,256]{1,0:T(8,128)(2,1)S(1)} %get-tuple-element.104.pair_kernel), custom_call_target="tpu_custom_call" | custom-call | tf_op jit(solution)/shard_map/cond/branch_0_fun/pallas_call | solution.py:185
  39.5 0.7 %copy.47 = bf16[500,256]{1,0:T(8,128)(2,1)} copy(bf16[500,256]{1,0:T(8,128)(2,1)S(1)} %get-tuple-element.97) | data formatting | bytes 512000
Async XLA Ops:
  0.7 25.3 %copy-start = (bf16[256,256]{1,0:T(8,128)(2,1)S(1)}, bf16[256,256]{1,0:T(8,128)(2,1)}, u32[]{:S(2)}) copy-start(bf16[256,256]{1,0:T(8,128)(2,1)} %param.40) | copy-start | bytes 393220
  0.7 25.3 %copy-start.1 = (bf16[256,256]{1,0:T(8,128)(2,1)S(1)}, bf16[256,256]{1,0:T(8,128)(2,1)}, u32[]{:S(2)}) copy-start(bf16[256,256]{1,0:T(8,128)(2,1)} %param.41) | copy-start | bytes 393220
where the time goes:
time: 40 us; the launch traced here: 40.2 us
  Pallas kernels  38.6 us (96%)
  between operations  0.77 us (2%)
  local copies, waits for them, and re-layouts  0.71 us (2%)
    pallas_call x1, Pallas kernels, swap(): pl.pallas_call(functools.partial(swap_kernel, round_number, blocks), out_...  25.2 us
    pallas_call x1, Pallas kernels, finish(): pl.pallas_call(functools.partial(finish_kernel, shift, blocks, groups), o...  13.4 us

commit v1 on v0

v1 whole, which is shorter than its diff:
```python
import functools

import jax
import jax.numpy as jnp
from jax import lax
from jax.experimental import pallas as pl
from jax.experimental.pallas import tpu as pltpu
from jax.sharding import PartitionSpec as P

MESH = pl.DeviceIdType.MESH
VMEM = 56 * 1024 * 1024


def swap_kernel(round_number, blocks, orbitals, arrived, between, send_sem, recv_sem):
    me = lax.axis_index("pts")
    line = max(blocks // 8, 2)
    partner = lax.rem(round_number + blocks - me, blocks)
    row_mate = partner // line * line + lax.rem(me, line)
    place_mate = me // line * line + lax.rem(partner, line)
    moves = row_mate != me
    bands, points = orbitals.shape
    split = bands // 32 * 16
    width = points // 2
    pieces = [
        (pl.ds(first, size), pl.ds(column * width, width))
        for first, size in ((0, split), (split, bands - split))
        for column in range(2)
    ]
    mates = [row_mate, place_mate, row_mate, place_mate]

    barrier = pltpu.get_barrier_semaphore()
    pl.semaphore_signal(barrier, inc=1, device_id={"pts": place_mate}, device_id_type=MESH)

    @pl.when(moves)
    def _():
        pl.semaphore_signal(barrier, inc=1, device_id={"pts": row_mate}, device_id_type=MESH)

    def send(src, dst, piece, semaphore, mate):
        return pltpu.make_async_remote_copy(
            src_ref=src.at[piece],
            dst_ref=dst.at[piece],
            send_sem=send_sem.at[semaphore],
            recv_sem=recv_sem.at[semaphore],
            device_id={"pts": mate},
            device_id_type=MESH,
        )

    count = len(pieces)

    @pl.when(jnp.logical_not(moves))
    def _():
        pl.semaphore_wait(barrier, 1)
        copies = [
            send(orbitals, arrived, piece, count + k, place_mate) for k, piece in enumerate(pieces)
        ]
        for copy in copies:
            copy.start()
        for copy in copies:
            copy.wait()

    @pl.when(moves)
    def _():
        pl.semaphore_wait(barrier, 2)
        firsts = [
            send(orbitals, between, piece, k, mates[k]) for k, piece in enumerate(pieces)
        ]
        seconds = [
            send(between, arrived, piece, count + k, mates[k ^ 1]) for k, piece in enumerate(pieces)
        ]
        for copy in firsts:
            copy.start()
        for first, second in zip(firsts, seconds):
            first.wait_recv()
            second.start()
        for copy in firsts:
            copy.wait_send()
        for copy in seconds:
            copy.wait()


def swap(round_number, collective, blocks, orbitals):
    return pl.pallas_call(
        functools.partial(swap_kernel, round_number, blocks),
        out_shape=jax.ShapeDtypeStruct(orbitals.shape, orbitals.dtype),
        in_specs=[pl.BlockSpec(memory_space=pl.ANY)],
        out_specs=pl.BlockSpec(memory_space=pl.ANY),
        scratch_shapes=[
            pltpu.VMEM(orbitals.shape, orbitals.dtype),
            pltpu.SemaphoreType.DMA((8,)),
            pltpu.SemaphoreType.DMA((8,)),
        ],
        compiler_params=pltpu.CompilerParams(
            collective_id=collective, has_side_effects=True, vmem_limit_bytes=VMEM
        ),
    )(orbitals)


def finish_kernel(
    shift,
    blocks,
    groups,
    orbitals,
    swapped,
    self_kernel,
    pair_kernel,
    out,
    own,
    arrived,
    kernels,
    own_t,
    part,
    part_in,
    chip,
    chip_in,
    dens,
    total,
    local_sem,
    shift_sem,
    chip_send,
    chip_recv,
    link_send,
    link_recv,
    back_send,
    back_recv,
):
    me = lax.axis_index("pts")
    band = lax.axis_index("band")
    core = lax.rem(band, 2)
    sibling = {"band": band + 1 - 2 * core}
    across = {"band": lax.rem(band + 2, groups)}
    points = own.shape[1]
    rows = points // 2

    loads = [
        pltpu.make_async_copy(orbitals, own, local_sem.at[0]),
        pltpu.make_async_copy(self_kernel, kernels.at[0], local_sem.at[1]),
        pltpu.make_async_copy(pair_kernel, kernels.at[1], local_sem.at[2]),
    ]
    if not shift:
        loads.append(pltpu.make_async_copy(swapped, arrived, local_sem.at[3]))
    for load in loads:
        load.start()

    barrier = pltpu.get_barrier_semaphore()
    pl.semaphore_signal(barrier, inc=1, device_id=sibling, device_id_type=MESH)
    pl.semaphore_signal(barrier, inc=1, device_id=across, device_id_type=MESH)
    if shift:
        source = {"pts": lax.rem(me + blocks - shift, blocks)}
        pl.semaphore_signal(barrier, inc=1, device_id=source, device_id_type=MESH)
    pl.semaphore_wait(barrier, 3 if shift else 2)

    pending = []

    def send(src, dst, semaphores, target):
        copy = pltpu.make_async_remote_copy(
            src_ref=src,
            dst_ref=dst,
            send_sem=semaphores[0],
            recv_sem=semaphores[1],
            device_id=target,
            device_id_type=MESH,
        )
        copy.start()
        pending.append(copy)
        return copy

    def wide(value):
        return value.astype(jnp.float32)

    def narrow(value):
        return value.astype(jnp.bfloat16)

    def partial(stage, block):
        product = jnp.dot(own_t[...], block[...], preferred_element_type=jnp.float32)
        part[stage, 0] = narrow(product[:rows])
        part[stage, 1] = narrow(product[rows:])

    def start(at):
        return send(
            part.at[at, 1 - core], part_in.at[at], (chip_send.at[at], chip_recv.at[at]), sibling
        )

    def cross(at, copy):
        copy.wait_recv()
        chip[at] = narrow(wide(part[at, core]) + wide(part_in[at]))
        return send(chip.at[at], chip_in.at[at], (link_send.at[at], link_recv.at[at]), across)

    def back(at, copy):
        copy.wait_recv()
        dens[at, core] = narrow(wide(chip[at]) + wide(chip_in[at]))
        return send(
            dens.at[at, core], dens.at[at, core], (back_send.at[at], back_recv.at[at]), sibling
        )

    def apply(stage, block, copy):
        copy.wait_recv()
        density = dens[stage].reshape(points, points)
        weight = narrow(wide(kernels[stage]) * wide(density))
        return lax.dot_general(
            block[...], weight, (((1,), (1,)), ((), ())), preferred_element_type=jnp.float32
        )

    if shift:
        target = {"pts": lax.rem(me + shift, blocks)}
        moved = send(swapped, arrived, (shift_sem.at[0], shift_sem.at[1]), target)
    loads[0].wait()
    own_t[...] = own[...].T
    partial(0, own)
    first = start(0)
    if shift:
        first = cross(0, first)
        first = back(0, first)
        loads[1].wait()
        loads[2].wait()
        total[...] = apply(0, own, first)
        moved.wait_recv()
        partial(1, arrived)
        second = start(1)
        second = cross(1, second)
        second = back(1, second)
    else:
        loads[3].wait()
        partial(1, arrived)
        second = start(1)
        first = cross(0, first)
        second = cross(1, second)
        loads[1].wait()
        loads[2].wait()
        first = back(0, first)
        second = back(1, second)
        total[...] = apply(0, own, first)
    out[...] = (total[...] + apply(1, arrived, second)).astype(out.dtype)
    for copy in pending:
        copy.wait_send()


def finish(shift, collective, blocks, groups, orbitals, swapped, self_kernel, pair_kernel):
    bands, points = orbitals.shape
    rows = points // 2
    half = jnp.bfloat16
    dma = pltpu.SemaphoreType.DMA
    return pl.pallas_call(
        functools.partial(finish_kernel, shift, blocks, groups),
        out_shape=jax.ShapeDtypeStruct((bands, points), half),
        in_specs=[pl.BlockSpec(memory_space=pl.ANY)] * 4,
        out_specs=pl.BlockSpec(memory_space=pltpu.VMEM),
        scratch_shapes=[
            pltpu.VMEM((bands, points), half),
            pltpu.VMEM((bands, points), half),
            pltpu.VMEM((2, points, points), half),
            pltpu.VMEM((points, bands), half),
            pltpu.VMEM((2, 2, rows, points), half),
            pltpu.VMEM((2, rows, points), half),
            pltpu.VMEM((2, rows, points), half),
            pltpu.VMEM((2, rows, points), half),
            pltpu.VMEM((2, 2, rows, points), half),
            pltpu.VMEM((bands, points), jnp.float32),
            dma((4,)),
            dma((2,)),
            dma((2,)),
            dma((2,)),
            dma((2,)),
            dma((2,)),
            dma((2,)),
            dma((2,)),
        ],
        compiler_params=pltpu.CompilerParams(
            collective_id=collective, has_side_effects=True, vmem_limit_bytes=VMEM
        ),
    )(orbitals, swapped, self_kernel, pair_kernel)


def per_device(blocks, groups, orbitals, partner, self_kernel, pair_kernel):
    shift = max(blocks // 8, 2)
    pairs = shift // 2
    count = blocks // 4
    round_number = lax.rem(partner[0] + lax.axis_index("pts"), blocks)
    bit = lax.rem(round_number // shift, 2)
    index = round_number // (2 * shift) * pairs + lax.rem(round_number, shift) // 2
    swaps = [
        functools.partial(swap, 2 * shift * (k // pairs) + 2 * (k % pairs) + 1, k, blocks)
        for k in range(count)
    ]
    swapped = lax.switch(index, swaps, orbitals)
    return lax.cond(
        bit == 1,
        functools.partial(finish, shift, count, blocks, groups),
        functools.partial(finish, 0, count + 1, blocks, groups),
        orbitals,
        swapped,
        self_kernel,
        pair_kernel,
    )


def solution(mesh):
    return jax.shard_map(
        functools.partial(per_device, mesh.shape["pts"], mesh.shape["band"]),
        mesh=mesh,
        in_specs=(P("band", "pts"), P("pts"), P("pts", None), P("pts", None)),
        out_specs=P("band", "pts"),
        check_vma=False,
    )
```

time: 40 us -> 40.7 us (1.018)
  the two profiles are of different devices: /device:TPU:447 before, /device:TPU:25 now
where the time goes in v1:
time: 40.7 us; the launch traced here: 40.6 us
  Pallas kernels  39 us (96%)
  between operations  0.77 us (2%)
  local copies, waits for them, and re-layouts  0.71 us (2%)
    pallas_call x1, Pallas kernels, swap(): pl.pallas_call(functools.partial(swap_kernel, round_number, blocks), out_...  22.2 us
    pallas_call x1, Pallas kernels, finish(): pl.pallas_call(functools.partial(finish_kernel, shift, blocks, groups), o...  16.8 us

profile of v1, /device:TPU:25, one launch (start us, length us, event | category | flops | bytes accessed | tf_op | source)
XLA Modules:
  0.0 40.6 jit_solution(901315937687819867)
XLA Ops:
  0.7 0.0 copy-start
  0.7 0.0 copy-start.1
  0.7 22.3 %conditional.2 = (bf16[500,256]{1,0:T(8,128)(2,1)S(1)}) conditional(s32[]{:T(128)} %clamp.3, bf16[500,256]{1,0:T(8,128)(2,1)} %param.38, bf16[500,256]{1,0:T(8,128)(2,1)} %param.38, bf16[500,256]{1,0:T(8,128)(2,1)} %param.38, bf16[500,256]{1,0:T(8,128)(2,1)} %param.38, bf16[500,256]{1,0:T(8,128)(2,1)} %param.38, ...), branch_computations={%region_0.1_spmd, %region_1.2_spmd, %region_2.3_spmd, %region_3.4_... | conditional | bytes 8 | solution.py:284
  0.8 22.2 %branch_15_fun.1 = bf16[500,256]{1,0:T(8,128)(2,1)S(1)} custom-call(bf16[500,256]{1,0:T(8,128)(2,1)} %orbitals.15), custom_call_target="tpu_custom_call" | custom-call | tf_op jit(solution)/shard_map/cond/branch_15_fun/pallas_call | solution.py:82
  23.1 0.0 copy-done
  23.1 0.0 copy-done.1
  23.1 16.8 %conditional.3 = (bf16[500,256]{1,0:T(8,128)(2,1)S(1)}) conditional(s32[]{:T(128)} %convert_element_type.3, (bf16[500,256]{1,0:T(8,128)(2,1)}, bf16[500,256]{1,0:T(8,128)(2,1)S(1)}, bf16[256,256]{1,0:T(8,128)(2,1)S(1)}, bf16[256,256]{1,0:T(8,128)(2,1)S(1)}) %tuple.146, (bf16[500,256]{1,0:T(8,128)(2,1)}, bf16[500,256]{1,0:T(8,128)(2,1)S(1)}, ...), branch_computations={%region_32.33_spmd, %region_33.34_spmd} | conditional | bytes 8 | solution.py:285
  23.1 16.8 %branch_0_fun.3 = bf16[500,256]{1,0:T(8,128)(2,1)S(1)} custom-call(bf16[500,256]{1,0:T(8,128)(2,1)} %get-tuple-element.89.orbitals, bf16[500,256]{1,0:T(8,128)(2,1)S(1)} %get-tuple-element.90.swapped, bf16[256,256]{1,0:T(8,128)(2,1)S(1)} %get-tuple-element.102.self_kernel, bf16[256,256]{1,0:T(8,128)(2,1)S(1)} %get-tuple-element.104.pair_kernel), custom_call_target="tpu_custom_call" | custom-call | tf_op jit(solution)/shard_map/cond/branch_0_fun/pallas_call | solution.py:242
  39.9 0.7 %copy.47 = bf16[500,256]{1,0:T(8,128)(2,1)} copy(bf16[500,256]{1,0:T(8,128)(2,1)S(1)} %get-tuple-element.97) | data formatting | bytes 512000
Async XLA Ops:
  0.7 22.3 %copy-start = (bf16[256,256]{1,0:T(8,128)(2,1)S(1)}, bf16[256,256]{1,0:T(8,128)(2,1)}, u32[]{:S(2)}) copy-start(bf16[256,256]{1,0:T(8,128)(2,1)} %param.40) | copy-start | bytes 393220
  0.7 22.3 %copy-start.1 = (bf16[256,256]{1,0:T(8,128)(2,1)S(1)}, bf16[256,256]{1,0:T(8,128)(2,1)}, u32[]{:S(2)}) copy-start(bf16[256,256]{1,0:T(8,128)(2,1)} %param.41) | copy-start | bytes 393220

commit v2 on v1

--- a/solution.py
+++ b/solution.py
@@ -26,7 +26,10 @@
         for first, size in ((0, split), (split, bands - split))
         for column in range(2)
     ]
-    mates = [row_mate, place_mate, row_mate, place_mate]
+    odd = lax.rem(lax.axis_index("band"), 2) == 1
+    ahead = jnp.where(odd, place_mate, row_mate)
+    behind = jnp.where(odd, row_mate, place_mate)
+    mates = [ahead, behind, ahead, behind]
 
     barrier = pltpu.get_barrier_semaphore()
     pl.semaphore_signal(barrier, inc=1, device_id={"pts": place_mate}, device_id_type=MESH)
@@ -147,7 +150,8 @@
     if shift:
         source = {"pts": lax.rem(me + blocks - shift, blocks)}
         pl.semaphore_signal(barrier, inc=1, device_id=source, device_id_type=MESH)
-    pl.semaphore_wait(barrier, 3 if shift else 2)
+    if shift:
+        pl.semaphore_wait(barrier, 3)
 
     pending = []
 
@@ -206,6 +210,10 @@
     loads[0].wait()
     own_t[...] = own[...].T
     partial(0, own)
+    if not shift:
+        loads[3].wait()
+        partial(1, arrived)
+        pl.semaphore_wait(barrier, 2)
     first = start(0)
     if shift:
         first = cross(0, first)
@@ -219,8 +227,6 @@
         second = cross(1, second)
         second = back(1, second)
     else:
-        loads[3].wait()
-        partial(1, arrived)
         second = start(1)
         first = cross(0, first)
         second = cross(1, second)

time: 40.7 us -> 46.2 us (1.14)
  the two profiles are of different devices: /device:TPU:25 before, /device:TPU:3 now
where the time goes in v2:
time: 46.2 us; the launch traced here: 46.1 us
  Pallas kernels  44.5 us (96%)
  between operations  0.77 us (2%)
  local copies, waits for them, and re-layouts  0.71 us (2%)
    pallas_call x1, Pallas kernels, swap(): pl.pallas_call(functools.partial(swap_kernel, round_number, blocks), out_...  26.1 us
    pallas_call x1, Pallas kernels, finish(): pl.pallas_call(functools.partial(finish_kernel, shift, blocks, groups), o...  18.4 us

profile of v2, /device:TPU:3, one launch (start us, length us, event | category | flops | bytes accessed | tf_op | source)
XLA Modules:
  0.0 46.1 jit_solution(12576149572424382334)
XLA Ops:
  0.7 0.0 copy-start
  0.7 0.0 copy-start.1
  0.7 26.2 %conditional.2 = (bf16[500,256]{1,0:T(8,128)(2,1)S(1)}) conditional(s32[]{:T(128)} %clamp.3, bf16[500,256]{1,0:T(8,128)(2,1)} %param.38, bf16[500,256]{1,0:T(8,128)(2,1)} %param.38, bf16[500,256]{1,0:T(8,128)(2,1)} %param.38, bf16[500,256]{1,0:T(8,128)(2,1)} %param.38, bf16[500,256]{1,0:T(8,128)(2,1)} %param.38, ...), branch_computations={%region_0.1_spmd, %region_1.2_spmd, %region_2.3_spmd, %region_3.4_... | conditional | bytes 8 | solution.py:290
  0.8 26.1 %branch_1_fun.2 = bf16[500,256]{1,0:T(8,128)(2,1)S(1)} custom-call(bf16[500,256]{1,0:T(8,128)(2,1)} %orbitals.1), custom_call_target="tpu_custom_call" | custom-call | tf_op jit(solution)/shard_map/cond/branch_1_fun/pallas_call | solution.py:85
  26.9 0.0 copy-done
  27.0 0.0 copy-done.1
  27.0 18.4 %conditional.3 = (bf16[500,256]{1,0:T(8,128)(2,1)S(1)}) conditional(s32[]{:T(128)} %convert_element_type.3, (bf16[500,256]{1,0:T(8,128)(2,1)}, bf16[500,256]{1,0:T(8,128)(2,1)S(1)}, bf16[256,256]{1,0:T(8,128)(2,1)S(1)}, bf16[256,256]{1,0:T(8,128)(2,1)S(1)}) %tuple.146, (bf16[500,256]{1,0:T(8,128)(2,1)}, bf16[500,256]{1,0:T(8,128)(2,1)S(1)}, ...), branch_computations={%region_32.33_spmd, %region_33.34_spmd} | conditional | bytes 8 | solution.py:291
  27.0 18.4 %branch_1_fun.3 = bf16[500,256]{1,0:T(8,128)(2,1)S(1)} custom-call(bf16[500,256]{1,0:T(8,128)(2,1)} %get-tuple-element.93.orbitals, bf16[500,256]{1,0:T(8,128)(2,1)S(1)} %get-tuple-element.94.swapped, bf16[256,256]{1,0:T(8,128)(2,1)S(1)} %get-tuple-element.103.self_kernel, bf16[256,256]{1,0:T(8,128)(2,1)S(1)} %get-tuple-element.105.pair_kernel), custom_call_target="tpu_custom_call" | custom-call | tf_op jit(solution)/shard_map/cond/branch_1_fun/pallas_call | solution.py:248
  45.4 0.7 %copy.47 = bf16[500,256]{1,0:T(8,128)(2,1)} copy(bf16[500,256]{1,0:T(8,128)(2,1)S(1)} %get-tuple-element.97) | data formatting | bytes 512000
Async XLA Ops:
  0.7 26.2 %copy-start = (bf16[256,256]{1,0:T(8,128)(2,1)S(1)}, bf16[256,256]{1,0:T(8,128)(2,1)}, u32[]{:S(2)}) copy-start(bf16[256,256]{1,0:T(8,128)(2,1)} %param.40) | copy-start | bytes 393220
  0.7 26.2 %copy-start.1 = (bf16[256,256]{1,0:T(8,128)(2,1)S(1)}, bf16[256,256]{1,0:T(8,128)(2,1)}, u32[]{:S(2)}) copy-start(bf16[256,256]{1,0:T(8,128)(2,1)} %param.41) | copy-start | bytes 393220

commit v3 on v2

--- a/solution.py
+++ b/solution.py
@@ -174,68 +174,110 @@
     def narrow(value):
         return value.astype(jnp.bfloat16)
 
-    def partial(stage, block):
-        product = jnp.dot(own_t[...], block[...], preferred_element_type=jnp.float32)
-        part[stage, 0] = narrow(product[:rows])
-        part[stage, 1] = narrow(product[rows:])
-
-    def start(at):
+    def partial(stage, block, columns):
+        product = jnp.dot(own_t[...], block[:, columns], preferred_element_type=jnp.float32)
+        part[stage, 0, :, columns] = narrow(product[:rows])
+        part[stage, 1, :, columns] = narrow(product[rows:])
+
+    def start(at, stage, columns):
         return send(
-            part.at[at, 1 - core], part_in.at[at], (chip_send.at[at], chip_recv.at[at]), sibling
-        )
-
-    def cross(at, copy):
+            part.at[stage, 1 - core, :, columns],
+            part_in.at[stage, :, columns],
+            (chip_send.at[at], chip_recv.at[at]),
+            sibling,
+        )
+
+    def cross(at, stage, columns, copy):
         copy.wait_recv()
-        chip[at] = narrow(wide(part[at, core]) + wide(part_in[at]))
-        return send(chip.at[at], chip_in.at[at], (link_send.at[at], link_recv.at[at]), across)
-
-    def back(at, copy):
+        chip[stage, :, columns] = narrow(
+            wide(part[stage, core, :, columns]) + wide(part_in[stage, :, columns])
+        )
+        return send(
+            chip.at[stage, :, columns],
+            chip_in.at[stage, :, columns],
+            (link_send.at[at], link_recv.at[at]),
+            across,
+        )
+
+    def back(at, stage, columns, copy):
         copy.wait_recv()
-        dens[at, core] = narrow(wide(chip[at]) + wide(chip_in[at]))
+        dens[stage, core, :, columns] = narrow(
+            wide(chip[stage, :, columns]) + wide(chip_in[stage, :, columns])
+        )
         return send(
-            dens.at[at, core], dens.at[at, core], (back_send.at[at], back_recv.at[at]), sibling
-        )
-
-    def apply(stage, block, copy):
-        copy.wait_recv()
-        density = dens[stage].reshape(points, points)
-        weight = narrow(wide(kernels[stage]) * wide(density))
+            dens.at[stage, core, :, columns],
+            dens.at[stage, core, :, columns],
+            (back_send.at[at], back_recv.at[at]),
+            sibling,
+        )
+
+    def span(half):
+        return pl.ds(pl.multiple_of(half * rows, rows), rows)
+
+    def apply(stage, block, half):
+        weight = narrow(wide(kernels[stage, span(half)]) * wide(dens[stage, half]))
         return lax.dot_general(
             block[...], weight, (((1,), (1,)), ((), ())), preferred_element_type=jnp.float32
         )
 
+    def keep(half):
+        total[half] = apply(0, own, half)
+
+    def put(half):
+        out[:, span(half)] = (total[half] + apply(1, arrived, half)).astype(out.dtype)
+
+    whole = pl.ds(0, points)
+    halves = [pl.ds(0, rows), pl.ds(rows, rows)]
     if shift:
         target = {"pts": lax.rem(me + shift, blocks)}
-        moved = send(swapped, arrived, (shift_sem.at[0], shift_sem.at[1]), target)
+        moved = [
+            send(
+                swapped.at[:, columns],
+                arrived.at[:, columns],
+                (shift_sem.at[0, h], shift_sem.at[1, h]),
+                target,
+            )
+            for h, columns in enumerate(halves)
+        ]
     loads[0].wait()
     own_t[...] = own[...].T
-    partial(0, own)
+    partial(0, own, whole)
     if not shift:
         loads[3].wait()
-        partial(1, arrived)
+        partial(1, arrived, whole)
         pl.semaphore_wait(barrier, 2)
-    first = start(0)
+    first = start(0, 0, whole)
     if shift:
-        first = cross(0, first)
-        first = back(0, first)
+        first = cross(0, 0, whole, first)
+        first = back(0, 0, whole, first)
         loads[1].wait()
         loads[2].wait()
-        total[...] = apply(0, own, first)
-        moved.wait_recv()
-        partial(1, arrived)
-        second = start(1)
-        second = cross(1, second)
-        second = back(1, second)
+        keep(core)
+        first.wait_recv()
+        seconds = []
+        for h, columns in enumerate(halves):
+            moved[h].wait_recv()
+            partial(1, arrived, columns)
+            seconds.append(start(1 + h, 1, columns))
+            if h == 0:
+                keep(1 - core)
+        seconds = [cross(1 + h, 1, halves[h], copy) for h, copy in enumerate(seconds)]
+        seconds = [back(1 + h, 1, halves[h], copy) for h, copy in enumerate(seconds)]
     else:
-        second = start(1)
-        first = cross(0, first)
-        second = cross(1, second)
+        second = start(1, 1, whole)
+        first = cross(0, 0, whole, first)
+        second = cross(1, 1, whole, second)
         loads[1].wait()
         loads[2].wait()
-        first = back(0, first)
-        second = back(1, second)
-        total[...] = apply(0, own, first)
-    out[...] = (total[...] + apply(1, arrived, second)).astype(out.dtype)
+        first = back(0, 0, whole, first)
+        seconds = [back(1, 1, whole, second)]
+        keep(core)
+        first.wait_recv()
+        keep(1 - core)
+    put(core)
+    for copy in seconds:
+        copy.wait_recv()
+    put(1 - core)
     for copy in pending:
         copy.wait_send()
 
@@ -260,15 +302,15 @@
             pltpu.VMEM((2, rows, points), half),
             pltpu.VMEM((2, rows, points), half),
             pltpu.VMEM((2, 2, rows, points), half),
-            pltpu.VMEM((bands, points), jnp.float32),
+            pltpu.VMEM((2, bands, rows), jnp.float32),
             dma((4,)),
-            dma((2,)),
-            dma((2,)),
-            dma((2,)),
-            dma((2,)),
-            dma((2,)),
-            dma((2,)),
-            dma((2,)),
+            dma((2, 2)),
+            dma((3,)),
+            dma((3,)),
+            dma((3,)),
+            dma((3,)),
+            dma((3,)),
+            dma((3,)),
         ],
         compiler_params=pltpu.CompilerParams(
             collective_id=collective, has_side_effects=True, vmem_limit_bytes=VMEM
@@ -280,13 +322,20 @@
     shift = max(blocks // 8, 2)
     pairs = shift // 2
     count = blocks // 4
+
+    def upper(low):
+        return low // pairs if pairs > 1 else 0
+
     round_number = lax.rem(partner[0] + lax.axis_index("pts"), blocks)
-    bit = lax.rem(round_number // shift, 2)
-    index = round_number // (2 * shift) * pairs + lax.rem(round_number, shift) // 2
-    swaps = [
-        functools.partial(swap, 2 * shift * (k // pairs) + 2 * (k % pairs) + 1, k, blocks)
-        for k in range(count)
-    ]
+    low = lax.rem(round_number, shift)
+    high = round_number // shift
+    bit = lax.rem(high + upper(low), 2)
+    index = lax.rem(high + blocks // shift - bit, blocks // shift) // 2 * pairs + low // 2
+    swaps = []
+    for k in range(count):
+        base_low = 2 * (k % pairs) + 1
+        base_high = 2 * (k // pairs) + upper(base_low)
+        swaps.append(functools.partial(swap, shift * base_high + base_low, k, blocks))
     swapped = lax.switch(index, swaps, orbitals)
     return lax.cond(
         bit == 1,

time: 46.2 us -> 42.3 us (0.916)
  the two profiles are of different devices: /device:TPU:3 before, /device:TPU:1 now
where the time goes in v3:
time: 42.3 us; the launch traced here: 42.1 us
  Pallas kernels  40.5 us (96%)
  between operations  0.8 us (2%)
  local copies, waits for them, and re-layouts  0.71 us (2%)
    pallas_call x1, Pallas kernels, finish(): pl.pallas_call(functools.partial(finish_kernel, shift, blocks, groups), o...  21 us
    pallas_call x1, Pallas kernels, swap(): pl.pallas_call(functools.partial(swap_kernel, round_number, blocks), out_...  19.5 us

profile of v3, /device:TPU:1, one launch (start us, length us, event | category | flops | bytes accessed | tf_op | source)
XLA Modules:
  0.0 42.1 jit_solution(13658302566495756086)
XLA Ops:
  0.8 0.0 copy-start
  0.8 0.0 copy-start.1
  0.8 19.6 %conditional.2 = (bf16[500,256]{1,0:T(8,128)(2,1)S(1)}) conditional(s32[]{:T(128)} %clamp.3, bf16[500,256]{1,0:T(8,128)(2,1)} %param.38, bf16[500,256]{1,0:T(8,128)(2,1)} %param.38, bf16[500,256]{1,0:T(8,128)(2,1)} %param.38, bf16[500,256]{1,0:T(8,128)(2,1)} %param.38, bf16[500,256]{1,0:T(8,128)(2,1)} %param.38, ...), branch_computations={%region_0.1_spmd, %region_1.2_spmd, %region_2.3_spmd, %region_3.4_... | conditional | bytes 8 | solution.py:339
  0.8 19.5 %branch_4_fun.1 = bf16[500,256]{1,0:T(8,128)(2,1)S(1)} custom-call(bf16[500,256]{1,0:T(8,128)(2,1)} %orbitals.4), custom_call_target="tpu_custom_call" | custom-call | tf_op jit(solution)/shard_map/cond/branch_4_fun/pallas_call | solution.py:85
  20.3 0.0 copy-done
  20.4 0.0 copy-done.1
  20.4 21.1 %conditional.3 = (bf16[500,256]{1,0:T(8,128)(2,1)S(1)}) conditional(s32[]{:T(128)} %convert_element_type.3, (bf16[500,256]{1,0:T(8,128)(2,1)}, bf16[500,256]{1,0:T(8,128)(2,1)S(1)}, bf16[256,256]{1,0:T(8,128)(2,1)S(1)}, bf16[256,256]{1,0:T(8,128)(2,1)S(1)}) %tuple.146, (bf16[500,256]{1,0:T(8,128)(2,1)}, bf16[500,256]{1,0:T(8,128)(2,1)S(1)}, ...), branch_computations={%region_32.33_spmd, %region_33.34_spmd} | conditional | bytes 8 | solution.py:340
  20.4 21.0 %branch_1_fun.3 = bf16[500,256]{1,0:T(8,128)(2,1)S(1)} custom-call(bf16[500,256]{1,0:T(8,128)(2,1)} %get-tuple-element.93.orbitals, bf16[500,256]{1,0:T(8,128)(2,1)S(1)} %get-tuple-element.94.swapped, bf16[256,256]{1,0:T(8,128)(2,1)S(1)} %get-tuple-element.103.self_kernel, bf16[256,256]{1,0:T(8,128)(2,1)S(1)} %get-tuple-element.105.pair_kernel), custom_call_target="tpu_custom_call" | custom-call | tf_op jit(solution)/shard_map/cond/branch_1_fun/pallas_call | solution.py:290
  41.4 0.7 %copy.47 = bf16[500,256]{1,0:T(8,128)(2,1)} copy(bf16[500,256]{1,0:T(8,128)(2,1)S(1)} %get-tuple-element.97) | data formatting | bytes 512000
Async XLA Ops:
  0.8 19.6 %copy-start = (bf16[256,256]{1,0:T(8,128)(2,1)S(1)}, bf16[256,256]{1,0:T(8,128)(2,1)}, u32[]{:S(2)}) copy-start(bf16[256,256]{1,0:T(8,128)(2,1)} %param.40) | copy-start | bytes 393220
  0.8 19.6 %copy-start.1 = (bf16[256,256]{1,0:T(8,128)(2,1)S(1)}, bf16[256,256]{1,0:T(8,128)(2,1)}, u32[]{:S(2)}) copy-start(bf16[256,256]{1,0:T(8,128)(2,1)} %param.41) | copy-start | bytes 393220
